TPU v7x, 32 devices: a whole 2x2x4 slice. The times are simulated.
32 devices in a mesh: groups: 2 (over y), row: 4 (over z), chan: 2 (over x), sub: 2 (over core).
Axes of the slice: x: 2, y: 2, z: 4, core: 2. Of those that a mesh axis runs over, the one named last changes fastest.
Arguments:
- pair: bfloat16 [384, 192, 128], P(('groups', 'row'), ('chan', 'sub')), parts along dimension 0, may hold values from -6 to 6
- chain_len: int32 [8], P('groups'), parts along dimension 0, may hold values from 1 to 48, 144 in all
- norm_gain: float32 [128], replicated, may hold values from 0.1 to 1.9
- norm_bias: float32 [128], replicated, may hold values from -3 to 3
- left_proj: bfloat16 [128, 128], replicated, may hold values from -0.5 to 0.5
- left_gate: bfloat16 [128, 128], replicated, may hold values from -0.5 to 0.5
- right_proj: bfloat16 [128, 128], replicated, may hold values from -0.5 to 0.5
- right_gate: bfloat16 [128, 128], replicated, may hold values from -0.5 to 0.5
- out_norm_gain: float32 [128], replicated, may hold values from 0.1 to 1.9
- out_norm_bias: float32 [128], replicated, may hold values from -3 to 3
- out_proj: bfloat16 [128, 128], replicated, may hold values from -0.5 to 0.5
- out_gate: bfloat16 [128, 128], replicated, may hold values from -0.5 to 0.5
Outputs:
- relaid: bfloat16 [384, 192, 128], P('groups', ('chan', 'sub', 'row')), parts along dimension 0
There are 2 independent parts, one for each index of `groups`. A program takes and returns all parts, laid end to end along the dimension named above; an argument that names none is the same for every part. Nothing has to cross between parts.
Inputs may be any that keep to these rules, and one draw needn't show every extreme that they name: Chain c occupies residues c * (48) onward; its first chain_len[c] residues are valid. The entries sum to 144 and one of them equals 48.
All inputs are finite; a program needn't handle non-finite values.
Results may differ from a plain program's by a relative error of at most 0.0038.
Values may be sent and summed in bfloat16 or wider, within the bound.
A program may use at most 64 MiB of HBM per device.

v0:
```python
import jax
import jax.numpy as jnp
from jax import lax
from jax.sharding import PartitionSpec as P

EPS = 1e-05


def layer_norm(values, gain, bias, axis):
    mean = jnp.mean(values, axis=axis, keepdims=True)
    centred = values - mean
    spread = jnp.mean(centred * centred, axis=axis, keepdims=True)
    return centred * lax.rsqrt(spread + EPS) * gain + bias


def residue_valid(positions, chain_len, slot):
    owner = positions // slot
    picks = owner[:, None] == jnp.arange(chain_len.shape[0], dtype=jnp.int32)[None, :]
    limit = jnp.sum(jnp.where(picks, chain_len[None, :], 0), axis=1)
    return (positions % slot < limit).astype(jnp.float32)


def finish(base_flat, base_normed, tri_flat, out_norm_gain, out_norm_bias, out_proj, out_gate):
    gate = jax.nn.sigmoid(jnp.dot(base_normed, out_gate, preferred_element_type=jnp.float32))
    tri_normed = layer_norm(
        tri_flat.astype(jnp.float32), out_norm_gain[:, None], out_norm_bias[:, None], 0
    ).astype(jnp.bfloat16)
    update = jnp.einsum("hp,hc->pc", tri_normed, out_proj, preferred_element_type=jnp.float32)
    return (base_flat.astype(jnp.float32) + gate * update).astype(jnp.bfloat16)


def shards(
    pair,
    chain_len,
    norm_gain,
    norm_bias,
    left_proj,
    left_gate,
    right_proj,
    right_gate,
    out_norm_gain,
    out_norm_bias,
    out_proj,
    out_gate,
):
    rows, width, chans = pair.shape
    hidden = left_proj.shape[1]
    row_count = lax.axis_size("row")
    total = rows * row_count
    slot = total // chain_len.shape[0]
    column_block = lax.axis_index("chan") * lax.axis_size("sub") + lax.axis_index("sub")
    row_ids = lax.axis_index("row") * rows + jnp.arange(rows, dtype=jnp.int32)
    col_ids = column_block * width + jnp.arange(width, dtype=jnp.int32)
    row_valid = residue_valid(row_ids, chain_len, slot)
    col_valid = residue_valid(col_ids, chain_len, slot)
    flat = pair.reshape(rows * width, chans)
    normed = layer_norm(flat.astype(jnp.float32), norm_gain, norm_bias, 1).astype(jnp.bfloat16)
    w_in = jnp.concatenate([left_proj, left_gate, right_proj, right_gate], axis=1)
    projected = jnp.einsum("pc,cf->fp", normed, w_in, preferred_element_type=jnp.float32)
    weight = (row_valid[:, None] * col_valid[None, :]).reshape(1, rows * width)
    left_t = (
        (weight * jax.nn.sigmoid(projected[hidden : 2 * hidden]) * projected[:hidden])
        .astype(jnp.bfloat16)
        .reshape(hidden, rows, width)
    )
    right_t = (
        (weight * jax.nn.sigmoid(projected[3 * hidden :]) * projected[2 * hidden : 3 * hidden])
        .astype(jnp.bfloat16)
        .reshape(hidden, rows, width)
    )
    left_c, right_c = (
        lax.all_to_all(left_t, ("chan", "sub"), split_axis=0, concat_axis=2, tiled=True),
        lax.all_to_all(right_t, ("chan", "sub"), split_axis=0, concat_axis=2, tiled=True),
    )
    tri = jnp.einsum(
        "cik,cjk->cij",
        left_c,
        lax.all_gather(right_c, "row", axis=1, tiled=True),
        preferred_element_type=jnp.float32,
    ).astype(jnp.bfloat16)
    back = lax.all_to_all(tri, ("chan", "sub"), split_axis=2, concat_axis=0, tiled=True)
    tri_flat = back.reshape(hidden, rows * width)
    result = finish(flat, normed, tri_flat, out_norm_gain, out_norm_bias, out_proj, out_gate)
    relaid = lax.all_to_all(
        result.reshape(rows, width, chans), "row", split_axis=1, concat_axis=0, tiled=True
    )
    return relaid


def solution(mesh):
    return jax.shard_map(
        shards,
        mesh=mesh,
        in_specs=(
            P(("groups", "row"), ("chan", "sub"), None),
            P("groups"),
            P(),
            P(),
            P(),
            P(),
            P(),
            P(),
            P(),
            P(),
            P(),
            P(),
        ),
        out_specs=P("groups", ("chan", "sub", "row"), None),
        check_vma=False,
    )
```

profile of v0, /device:TPU:0, one launch (start us, length us, event | category | flops | bytes accessed | tf_op | source)
XLA Modules:
  0.0 158.4 jit_solution(11356723506418131942)
XLA Ops:
  6.6 1.5 convert_reduce_fusion
  8.2 1.8 %multiply_reduce_fusion.1 = f32[48,48]{1,0:T(8,128)S(1)} fusion(bf16[48,48,128]{2,1,0:T(8,128)(2,1)} %param.12, f32[48,48]{1,0:T(8,128)S(1)} %broadcast_multiply_fusion.2), kind=kLoop, calls=%fused_computation.29 | loop fusion | flops 1177344 | bytes 608256 | tf_op jit(solution)/shard_map/reduce_sum | solution.py:12
  10.4 1.3 fusion.18
  13.4 1.4 fusion.5
  16.1 2.7 %reshape.161 = bf16[4,2,36864]{2,1,0:T(2,128)(2,1)S(1)} reshape(bf16[128,48,48]{2,1,0:T(8,128)(2,1)S(1)} %copy.45) | data formatting | bytes 1179648
  18.8 13.6 %all_to_all.63 = bf16[4,2,36864]{2,1,0:T(2,128)(2,1)S(1)} all-to-all(bf16[4,2,36864]{2,1,0:T(2,128)(2,1)S(1)} %reshape.161), channel_id=1, replica_groups=mesh['groups'=2,'row'=4,'chan'=2,'sub'=2] {'chan','sub'}, dimensions={0} | all-to-all | bytes 1179648 | tf_op jit(solution)/shard_map/all_to_all | solution.py:73
  32.4 1.5 reshape.162
  33.9 1.2 copy.46
  35.1 1.6 %all_to_all.53 = bf16[32,48,192]{2,1,0:T(8,128)(2,1)} reshape(bf16[32,48,4,48]{3,2,1,0:T(4,128)(2,1)S(1)} %copy.46) | data formatting | bytes 1179648 | tf_op jit(solution)/shard_map/all_to_all | solution.py:73
  38.0 2.7 %reshape.159 = bf16[4,2,36864]{2,1,0:T(2,128)(2,1)S(1)} reshape(bf16[128,48,48]{2,1,0:T(8,128)(2,1)S(1)} %copy.42) | data formatting | bytes 1179648
  40.7 11.9 %all_to_all.64 = bf16[4,2,36864]{2,1,0:T(2,128)(2,1)S(1)} all-to-all(bf16[4,2,36864]{2,1,0:T(2,128)(2,1)S(1)} %reshape.159), channel_id=1, replica_groups=mesh['groups'=2,'row'=4,'chan'=2,'sub'=2] {'chan','sub'}, dimensions={0} | all-to-all | bytes 1179648 | tf_op jit(solution)/shard_map/all_to_all | solution.py:72
  52.6 1.5 reshape.160
  56.3 44.4 %all-gather.2.cloned.1.call-done = bf16[32,192,192]{2,1,0:T(8,128)(2,1)} async-done(((bf16[32,48,192]{2,1,0:T(8,128)(2,1)}), bf16[32,192,192]{2,1,0:T(8,128)(2,1)}) %all-gather.2.cloned.1.call-update) | async-done | bytes 2359312 | tf_op jit(solution)/shard_map/all_gather | solution.py:78
  100.7 3.0 %convolution_convert_fusion = bf16[32,48,192]{2,1,0:T(8,128)(2,1)S(1)} fusion(bf16[32,48,192]{2,1,0:T(8,128)(2,1)S(1)} %all_to_all.49, bf16[32,192,192]{2,1,0:T(8,128)(2,1)} %all-gather.2.cloned.1.call-done), kind=kOutput, calls=%fused_computation.8 | convolution fusion | flops 113541120 | bytes 3538944 | tf_op jit(solution)/shard_map/cik,cjk->cij/dot_general | solution.py:75
  103.7 1.4 copy.47
  105.2 3.4 %reshape.163 = bf16[4,2,36864]{2,1,0:T(2,128)(2,1)} reshape(bf16[192,32,48]{2,1,0:T(8,128)(2,1)S(1)} %bitcast.43) | data formatting | bytes 1179648
  108.5 3.5 %all-to-all-start.2 = ((bf16[4,2,36864]{2,1,0:T(2,128)(2,1)}), bf16[4,2,36864]{2,1,0:T(2,128)(2,1)S(1)}, u32[]{:S(2)}, u32[]{:S(2)}) async-start(bf16[4,2,36864]{2,1,0:T(2,128)(2,1)} %reshape.163), calls=%async_computation.2 | async-start | bytes 1179648 | tf_op jit(solution)/shard_map/all_to_all | solution.py:81
  112.0 1.5 fusion.3
  113.5 8.0 %all-to-all-done.2 = bf16[4,2,36864]{2,1,0:T(2,128)(2,1)S(1)} async-done(((bf16[4,2,36864]{2,1,0:T(2,128)(2,1)}), bf16[4,2,36864]{2,1,0:T(2,128)(2,1)S(1)}, u32[]{:S(2)}, u32[]{:S(2)}) %all-to-all-start.2) | async-done | bytes 589856 | tf_op jit(solution)/shard_map/all_to_all | solution.py:81
  121.5 2.4 %reshape.164 = bf16[192,32,48]{2,1,0:T(8,128)(2,1)} reshape(bf16[4,2,36864]{2,1,0:T(2,128)(2,1)S(1)} %all-to-all-done.2) | data formatting | bytes 1179648
  124.0 2.8 %copy.48 = f32[32,48,4,48]{3,1,0,2:T(8,128)S(1)} copy(bf16[32,48,4,48]{1,0,3,2:T(8,128)(2,1)} %bitcast.44) | data formatting | bytes 1769472 | tf_op jit(solution)/shard_map/convert_element_type | solution.py:26
  127.7 2.2 %reshape.156 = f32[128,2304]{1,0:T(8,128)} reshape(f32[4,32,48,48]{3,2,1,0:T(8,128)S(1)} %bitcast.39) | data formatting | bytes 2359296 | tf_op jit(solution)/shard_map/convert_element_type | solution.py:26
  129.9 2.2 %fusion.4 = bf16[2304,128]{1,0:T(8,128)(2,1)S(1)} fusion(f32[2304,128]{1,0:T(8,128)} %fusion.3, bf16[128,128]{1,0:T(8,128)(2,1)S(1)} %copy-done.9, f32[128,2304]{1,0:T(8,128)} %reshape.156, f32[128]{0:T(128)S(1)} %copy-done.12, f32[128]{0:T(128)S(1)} %copy-done.13, f32[2304]{0:T(1024)S(1)} %rsqrt.25, f32[2304]{0:T(1024)S(1)} %div.52, ...), kind=kOutput, calls=%fused_computation.6 | convolution fusion | flops 78151680 | bytes 3591168 | tf_op jit(solution)/shard_map/hp,hc->pc/dot_general | solution.py:28
  132.3 18.4 %all_to_all.65 = bf16[48,48,128]{2,0,1:T(8,128)(2,1)S(1)} all-to-all(bf16[48,48,128]{2,0,1:T(8,128)(2,1)S(1)} %copy.49), channel_id=1, replica_groups=mesh['groups'=2,'row'=4,'chan'=2,'sub'=2] {'row'}, dimensions={1} | all-to-all | bytes 1179648 | tf_op jit(solution)/shard_map/all_to_all | solution.py:84
  (57 shorter events, 8.7 us)
Async XLA Ops:
  6.5 105.5 %copy-start = (bf16[128,128]{1,0:T(8,128)(2,1)S(1)}, bf16[128,128]{1,0:T(8,128)(2,1)}, u32[]{:S(2)}) copy-start(bf16[128,128]{1,0:T(8,128)(2,1)} %param.23) | copy-start | bytes 98308
  6.5 3.9 %copy-start.1 = (bf16[48,48,128]{2,1,0:T(8,128)(2,1)S(1)}, bf16[48,48,128]{2,1,0:T(8,128)(2,1)}, u32[]{:S(2)}) copy-start(bf16[48,48,128]{2,1,0:T(8,128)(2,1)} %param.12) | copy-start | bytes 1769476
  6.5 3.5 %copy-start.14 = (s32[4]{0:T(128)S(1)}, s32[4]{0:T(128)}, u32[]{:S(2)}) copy-start(s32[4]{0:T(128)} %param.13) | copy-start | bytes 52
  6.5 3.9 %copy-start.11 = (f32[128]{0:T(128)S(1)}, f32[128]{0:T(128)}, u32[]{:S(2)}) copy-start(f32[128]{0:T(128)} %param.14) | copy-start | bytes 1540
  6.5 3.9 %copy-start.10 = (f32[128]{0:T(128)S(1)}, f32[128]{0:T(128)}, u32[]{:S(2)}) copy-start(f32[128]{0:T(128)} %param.15) | copy-start | bytes 1540
  6.5 94.1 %all-gather.2.cloned.1.call-start = ((), (), s32[]{:S(2)}) async-start(), calls=%async_computation.4 | async-start | bytes 3932160 | tf_op jit(solution)/shard_map/all_gather | solution.py:78
  8.1 4.5 %copy-start.5 = (bf16[128,128]{1,0:T(8,128)(2,1)S(1)}, bf16[128,128]{1,0:T(8,128)(2,1)}, u32[]{:S(2)}) copy-start(bf16[128,128]{1,0:T(8,128)(2,1)} %param.19) | copy-start | bytes 98308
  8.1 4.5 %copy-start.6 = (bf16[128,128]{1,0:T(8,128)(2,1)S(1)}, bf16[128,128]{1,0:T(8,128)(2,1)}, u32[]{:S(2)}) copy-start(bf16[128,128]{1,0:T(8,128)(2,1)} %param.18) | copy-start | bytes 98308
  8.1 4.5 %copy-start.7 = (bf16[128,128]{1,0:T(8,128)(2,1)S(1)}, bf16[128,128]{1,0:T(8,128)(2,1)}, u32[]{:S(2)}) copy-start(bf16[128,128]{1,0:T(8,128)(2,1)} %param.17) | copy-start | bytes 98308
  8.1 4.5 %copy-start.8 = (bf16[128,128]{1,0:T(8,128)(2,1)S(1)}, bf16[128,128]{1,0:T(8,128)(2,1)}, u32[]{:S(2)}) copy-start(bf16[128,128]{1,0:T(8,128)(2,1)} %param.16) | copy-start | bytes 98308
  11.8 0.8 copy-start.3
  35.1 1.6 %copy-start.2 = (bf16[128,2304]{1,0:T(8,128)(2,1)S(1)}, bf16[128,2304]{1,0:T(8,128)(2,1)}, u32[]{:S(2)}) copy-start(bf16[128,2304]{1,0:T(8,128)(2,1)} %get-tuple-element.8) | copy-start | bytes 1769476
  105.1 6.9 %copy-start.4 = (bf16[2304,128]{1,0:T(8,128)(2,1)S(1)}, bf16[2304,128]{1,0:T(8,128)(2,1)}, u32[]{:S(2)}) copy-start(bf16[2304,128]{1,0:T(8,128)(2,1)} %copy-done.3) | copy-start | bytes 1769476
  108.5 13.0 %all-to-all-start.2 = ((bf16[4,2,36864]{2,1,0:T(2,128)(2,1)}), bf16[4,2,36864]{2,1,0:T(2,128)(2,1)S(1)}, u32[]{:S(2)}, u32[]{:S(2)}) async-start(bf16[4,2,36864]{2,1,0:T(2,128)(2,1)} %reshape.163), calls=%async_computation.2 | async-start | bytes 1179648 | tf_op jit(solution)/shard_map/all_to_all | solution.py:81
  127.7 2.2 %copy-start.9 = (bf16[128,128]{1,0:T(8,128)(2,1)S(1)}, bf16[128,128]{1,0:T(8,128)(2,1)}, u32[]{:S(2)}) copy-start(bf16[128,128]{1,0:T(8,128)(2,1)} %param.22) | copy-start | bytes 98308
  127.7 2.2 %copy-start.12 = (f32[128]{0:T(128)S(1)}, f32[128]{0:T(128)}, u32[]{:S(2)}) copy-start(f32[128]{0:T(128)} %param.21) | copy-start | bytes 1540
  127.7 2.2 %copy-start.13 = (f32[128]{0:T(128)S(1)}, f32[128]{0:T(128)}, u32[]{:S(2)}) copy-start(f32[128]{0:T(128)} %param.20) | copy-start | bytes 1540
Sparse Core Ops, SparseCore 0:
  36.9 63.7 all-gather.1
where the time goes:
time: 159 us; the launch traced here: 158 us
  waiting for transfers between devices  52.4 us (33%)
  blocking collectives  43.9 us (28%)
  local copies, waits for them, and re-layouts  30.4 us (19%)
  between operations  13.7 us (9%)
  matrix products  7.49 us (5%)
  other arithmetic  7 us (4%)
  starting transfers between devices  3.51 us (2%)
    all_gather x1, waiting for transfers between devices, shards(): lax.all_gather(right_c, 'row', axis=1, tiled=True)  44.4 us
    all_to_all x1, blocking collectives, shards(): lax.all_to_all(result.reshape(rows, width, chans), 'row', split_axis=1, c...  18.4 us
    unnamed x36, local copies, waits for them, and re-layouts  15.1 us
    all_to_all x1, blocking collectives, shards(): lax.all_to_all(right_t, ('chan', 'sub'), split_axis=0, concat_axis=2, til...  13.6 us
    all_to_all x1, blocking collectives, shards(): lax.all_to_all(left_t, ('chan', 'sub'), split_axis=0, concat_axis=2, tile...  11.9 us
    all_to_all x1, waiting for transfers between devices, shards(): lax.all_to_all(tri, ('chan', 'sub'), split_axis=2, concat_axis=0, tiled=T...  8.01 us
    convert_element_type x2, local copies, waits for them, and re-layouts, finish(): tri_flat.astype(jnp.float32)  5.03 us
    all_to_all x1, starting transfers between devices, shards(): lax.all_to_all(tri, ('chan', 'sub'), split_axis=2, concat_axis=0, tiled=T...  3.48 us
  transfers between devices with their start and end apart: 2, of which 2 were waited for; matrix products, arithmetic and copies ran while one was open for 5% of the time, Pallas kernels for 0%

commit v1 on v0

--- a/solution.py
+++ b/solution.py
@@ -1,6 +1,10 @@
+import functools
+
 import jax
 import jax.numpy as jnp
 from jax import lax
+from jax.experimental import pallas as pl
+from jax.experimental.pallas import tpu as pltpu
 from jax.sharding import PartitionSpec as P
 
 EPS = 1e-05
@@ -29,7 +33,7 @@
     return (base_flat.astype(jnp.float32) + gate * update).astype(jnp.bfloat16)
 
 
-def shards(
+def shards_general(
     pair,
     chain_len,
     norm_gain,
@@ -87,6 +91,281 @@
     return relaid
 
 
+MESH = pl.DeviceIdType.MESH
+
+
+def place(rows, chans, subs):
+    row, chan, sub = lax.axis_index("row"), lax.axis_index("chan"), lax.axis_index("sub")
+    return (row * chans + chan) * subs + sub
+
+
+def coords(member, chans, subs):
+    return {
+        "row": member // (chans * subs),
+        "chan": (member // subs) % chans,
+        "sub": member % subs,
+    }
+
+
+def greet(me, count, chans, subs):
+    barrier = pltpu.get_barrier_semaphore()
+    for step in range(1, count):
+        peer = lax.rem(me + step, count)
+        pl.semaphore_signal(
+            barrier, inc=1, device_id=coords(peer, chans, subs), device_id_type=MESH
+        )
+    pl.semaphore_wait(barrier, count - 1)
+
+
+def norm_rows(values, gain, bias):
+    mean = jnp.mean(values, axis=1, keepdims=True)
+    centred = values - mean
+    spread = jnp.mean(centred * centred, axis=1, keepdims=True)
+    return centred * lax.rsqrt(spread + EPS) * gain + bias
+
+
+def norm_columns(values, gain, bias):
+    mean = jnp.mean(values, axis=0, keepdims=True)
+    centred = values - mean
+    spread = jnp.mean(centred * centred, axis=0, keepdims=True)
+    return centred * lax.rsqrt(spread + EPS) * gain + bias
+
+
+def sides_kernel(
+    dims, step_columns, pair, weight, gain, bias, w_in, got, moved, out, w_t, sems, pair_sems, own_sems
+):
+    rows, chans, subs = dims
+    count = rows * chans * subs
+    me = place(rows, chans, subs)
+    greet(me, count, chans, subs)
+    width, height, depth = pair.shape
+    share = width // rows
+    my_row = lax.axis_index("row")
+    pending = []
+    own_pair = pltpu.make_async_copy(
+        pair.at[pl.ds(my_row * share, share)],
+        moved.at[:, pl.ds(pl.multiple_of(my_row * height, height), height)],
+        own_sems.at[0],
+    )
+    own_pair.start()
+    pending.append(own_pair)
+    for step in range(1, rows):
+        target = lax.rem(my_row + step, rows)
+        copy = pltpu.make_async_remote_copy(
+            src_ref=pair.at[pl.ds(target * share, share)],
+            dst_ref=moved.at[:, pl.ds(pl.multiple_of(my_row * height, height), height)],
+            send_sem=pair_sems.at[0, step],
+            recv_sem=pair_sems.at[1, step],
+            device_id={"row": target},
+            device_id_type=MESH,
+        )
+        copy.start()
+        pending.append(copy)
+    hidden = w_in.shape[1] // 4
+    w_t[...] = w_in[...].astype(jnp.float32).T.astype(jnp.bfloat16)
+    lanes = step_columns * height
+    per = hidden // count
+
+    def body(index, carry):
+        block = pair[pl.ds(index * step_columns, step_columns)]
+        flat = block.astype(jnp.float32).reshape(lanes, depth)
+        normed = norm_rows(flat, gain[...], bias[...]).astype(jnp.bfloat16)
+        projected = lax.dot_general(
+            w_t[...], normed, (((1,), (1,)), ((), ())), preferred_element_type=jnp.float32
+        )
+        span = pl.ds(pl.multiple_of(index * lanes, 128), lanes)
+        valid = weight[:, span]
+        left = valid * jax.nn.sigmoid(projected[hidden : 2 * hidden]) * projected[:hidden]
+        right = (
+            valid * jax.nn.sigmoid(projected[3 * hidden :]) * projected[2 * hidden : 3 * hidden]
+        )
+        both = jnp.concatenate(
+            [left.reshape(count, per, lanes), right.reshape(count, per, lanes)], axis=1
+        )
+        out[:, :, span] = both.astype(jnp.bfloat16)
+        return carry
+
+    lax.fori_loop(0, width // step_columns, body, 0)
+    own = pltpu.make_async_copy(out.at[me], got.at[me], own_sems.at[1])
+    own.start()
+    pending.append(own)
+    for step in range(1, count):
+        peer = lax.rem(me + step, count)
+        copy = pltpu.make_async_remote_copy(
+            src_ref=out.at[peer],
+            dst_ref=got.at[me],
+            send_sem=sems.at[0, step],
+            recv_sem=sems.at[1, step],
+            device_id=coords(peer, chans, subs),
+            device_id_type=MESH,
+        )
+        copy.start()
+        pending.append(copy)
+    for copy in pending:
+        copy.wait()
+
+
+def finish_kernel(
+    dims, step_lanes, out, moved, gain, bias, out_gain, out_bias, proj, gate_w, result, got, sems, own_sem
+):
+    rows, chans, subs = dims
+    count = rows * chans * subs
+    me = place(rows, chans, subs)
+    greet(me, count, chans, subs)
+
+    def block_of(member):
+        return (member % (chans * subs)) * rows + member // (chans * subs)
+
+    own = pltpu.make_async_copy(out.at[block_of(me)], got.at[me], own_sem)
+    own.start()
+    pending = [own]
+    for step in range(1, count):
+        peer = lax.rem(me + step, count)
+        copy = pltpu.make_async_remote_copy(
+            src_ref=out.at[block_of(peer)],
+            dst_ref=got.at[me],
+            send_sem=sems.at[0, step],
+            recv_sem=sems.at[1, step],
+            device_id=coords(peer, chans, subs),
+            device_id_type=MESH,
+        )
+        copy.start()
+        pending.append(copy)
+    for copy in pending:
+        copy.wait()
+    half = got.shape[2]
+    per = got.shape[1] // 2
+    depth = moved.shape[1]
+
+    def body(index, carry):
+        lanes = pl.ds(pl.multiple_of(index * step_lanes, 128), step_lanes)
+        tri = got[:, :, lanes].astype(jnp.float32)
+        for part in range(2):
+            piece = tri[:, part * per : (part + 1) * per].reshape(count * per, step_lanes)
+            tri_normed = norm_columns(piece, out_gain[...], out_bias[...]).T.astype(jnp.bfloat16)
+            update = jnp.dot(tri_normed, proj[...], preferred_element_type=jnp.float32)
+            span = pl.ds(pl.multiple_of(part * half + index * step_lanes, 128), step_lanes)
+            base = moved[span, :].astype(jnp.float32)
+            normed = norm_rows(base, gain[...], bias[...]).astype(jnp.bfloat16)
+            gate = jax.nn.sigmoid(jnp.dot(normed, gate_w[...], preferred_element_type=jnp.float32))
+            result[span, :] = (base + gate * update).astype(jnp.bfloat16)
+        return carry
+
+    lax.fori_loop(0, half // step_lanes, body, 0)
+
+
+def product(got, dims, per, width, height):
+    rows, chans, subs = dims
+    blocks = chans * subs
+    sides = got.reshape(rows, blocks, 2, per, width, height)
+    sides = sides.transpose(2, 3, 1, 4, 0, 5).reshape(2, per, blocks * width, rows * height)
+    tri = jnp.einsum(
+        "ckj,cki->cji", sides[1], sides[0], preferred_element_type=jnp.float32
+    ).astype(jnp.bfloat16)
+    count = rows * blocks
+    total = rows * height
+    share = total // count
+    tri = tri.reshape(per, count, 2, share // 2, total).transpose(1, 2, 0, 3, 4)
+    return tri.reshape(count, 2 * per, share // 2 * total)
+
+
+def shards_direct(
+    pair,
+    chain_len,
+    norm_gain,
+    norm_bias,
+    left_proj,
+    left_gate,
+    right_proj,
+    right_gate,
+    out_norm_gain,
+    out_norm_bias,
+    out_proj,
+    out_gate,
+):
+    height, width, depth = pair.shape
+    hidden = left_proj.shape[1]
+    dims = (lax.axis_size("row"), lax.axis_size("chan"), lax.axis_size("sub"))
+    count = dims[0] * dims[1] * dims[2]
+    per = hidden // count
+    total = height * dims[0]
+    slot = total // chain_len.shape[0]
+    column_block = lax.axis_index("chan") * lax.axis_size("sub") + lax.axis_index("sub")
+    row_ids = lax.axis_index("row") * height + jnp.arange(height, dtype=jnp.int32)
+    col_ids = column_block * width + jnp.arange(width, dtype=jnp.int32)
+    row_valid = residue_valid(row_ids, chain_len, slot)
+    col_valid = residue_valid(col_ids, chain_len, slot)
+    weight = (col_valid[:, None] * row_valid[None, :]).reshape(1, width * height)
+    turned = pair.transpose(1, 0, 2)
+    w_in = jnp.concatenate([left_proj, left_gate, right_proj, right_gate], axis=1)
+    whole = pl.BlockSpec(memory_space=pltpu.VMEM)
+    share = width // dims[0]
+    got, moved = pl.pallas_call(
+        functools.partial(sides_kernel, dims, 8),
+        out_shape=(
+            jax.ShapeDtypeStruct((count, 2 * per, width * height), jnp.bfloat16),
+            jax.ShapeDtypeStruct((share, total, depth), jnp.bfloat16),
+        ),
+        in_specs=[whole] * 5,
+        out_specs=(whole, whole),
+        scratch_shapes=[
+            pltpu.VMEM((count, 2 * per, width * height), jnp.bfloat16),
+            pltpu.VMEM((4 * hidden, depth), jnp.bfloat16),
+            pltpu.SemaphoreType.DMA((2, count)),
+            pltpu.SemaphoreType.DMA((2, dims[0])),
+            pltpu.SemaphoreType.DMA((2,)),
+        ],
+        compiler_params=pltpu.CompilerParams(
+            collective_id=0, has_side_effects=True, vmem_limit_bytes=32 << 20
+        ),
+        name="sides",
+    )(turned, weight, norm_gain[None, :], norm_bias[None, :], w_in)
+    tri = product(got, dims, per, width, height)
+    half = share * total // 2
+    result = pl.pallas_call(
+        functools.partial(finish_kernel, dims, 384),
+        out_shape=jax.ShapeDtypeStruct((share * total, depth), jnp.bfloat16),
+        in_specs=[whole] * 8,
+        out_specs=whole,
+        scratch_shapes=[
+            pltpu.VMEM((count, 2 * per, half), jnp.bfloat16),
+            pltpu.SemaphoreType.DMA((2, count)),
+            pltpu.SemaphoreType.DMA,
+        ],
+        compiler_params=pltpu.CompilerParams(
+            collective_id=1, has_side_effects=True, vmem_limit_bytes=32 << 20
+        ),
+        name="finish",
+    )(
+        tri,
+        moved.reshape(share * total, depth),
+        norm_gain[None, :],
+        norm_bias[None, :],
+        out_norm_gain[:, None],
+        out_norm_bias[:, None],
+        out_proj,
+        out_gate,
+    )
+    return result.reshape(share, total, depth).transpose(1, 0, 2)
+
+
+def shards(pair, chain_len, *params):
+    height, width, _ = pair.shape
+    hidden = params[2].shape[1]
+    rows = lax.axis_size("row")
+    count = rows * lax.axis_size("chan") * lax.axis_size("sub")
+    fits = (
+        count * 8 == hidden
+        and height % 16 == 0
+        and width % (2 * rows) == 0
+        and (8 * height) % 128 == 0
+        and width % 8 == 0
+        and (width // rows * height * rows) % 768 == 0
+    )
+    body = shards_direct if fits else shards_general
+    return body(pair, chain_len, *params)
+
+
 def solution(mesh):
     return jax.shard_map(
         shards,

time: 159 us -> 89.6 us (0.56)
  the two profiles are of different devices: /device:TPU:0 before, /device:TPU:11 now
where the time goes in v1:
time: 89.6 us; the launch traced here: 89.3 us
  Pallas kernels  63.2 us (71%)
  local copies, waits for them, and re-layouts  22.7 us (25%)
  other arithmetic  1.69 us (2%)
  matrix products  1.49 us (2%)
    pallas_call x1, Pallas kernels, shards_direct(): pl.pallas_call(functools.partial(sides_kernel, dims, 8), out_shape=(jax.S...  43.4 us
    pallas_call x1, Pallas kernels, shards_direct(): pl.pallas_call(functools.partial(finish_kernel, dims, 384), out_shape=jax...  19.7 us
    slice x2, local copies, waits for them, and re-layouts, product(): sides[0]  7.06 us
    reshape x1, local copies, waits for them, and re-layouts, product(): sides = got.reshape(rows, blocks, 2, per, width, height)  5.25 us
    unnamed x18, local copies, waits for them, and re-layouts  3.38 us
    slice x1, local copies, waits for them, and re-layouts, product(): sides[1]  2.79 us

profile of v1, /device:TPU:11, one launch (start us, length us, event | category | flops | bytes accessed | tf_op | source)
XLA Modules:
  0.0 89.3 jit_solution(10151625327918107802)
XLA Ops:
  0.0 0.7 select_reduce_fusion.1
  0.8 0.1 broadcast_multiply_fusion
  0.9 0.1 mul.38.weight
  1.0 1.2 %copy.34 = bf16[48,48,128]{2,0,1:T(8,128)(2,1)S(1)} copy(bf16[48,48,128]{2,1,0:T(8,128)(2,1)} %param.12) | data formatting | bytes 1179648 | tf_op args[0]
  2.2 0.8 pad_maximum_fusion.w_in
  3.0 0.0 copy-start.2
  3.0 0.6 copy-done.2
  3.7 0.7 copy-done.4
  4.3 43.4 %sides.1 = (bf16[16,16,2304]{2,1,0:T(8,128)(2,1)S(1)}, bf16[12,192,128]{2,1,0:T(8,128)(2,1)S(1)}) custom-call(bf16[48,48,128]{2,1,0:T(8,128)(2,1)S(1)} %bitcast.20, f32[1,2304]{1,0:T(1,128)S(1)} %mul.38.weight, f32[1,128]{1,0:T(1,128)S(1)} %bitcast.22, f32[1,128]{1,0:T(1,128)S(1)} %bitcast.24, bf16[128,512]{1,0:T(8,128)(2,1)S(1)} %pad_maximum_fusion.w_in), custom_call_target="tpu_custom_call" | custom-call | tf_op jit(solution)/shard_map/sides/pallas_call | solution.py:303
  47.8 5.3 %reshape.92 = bf16[4,4,2,8,48,48]{5,4,3,2,1,0:T(8,128)(2,1)} reshape(bf16[16,16,2304]{2,1,0:T(8,128)(2,1)S(1)} %get-tuple-element.7) | data formatting | bytes 2359296 | tf_op jit(solution)/shard_map/reshape | solution.py:260
  53.0 4.4 %fusion.2 = (bf16[1,8,4,48,4,48]{5,3,1,0,2,4:T(8,128)(2,1)}, bf16[1,8,4,48,4,48]{5,3,1,0,2,4:T(8,128)(2,1)}) fusion(bf16[2,8,4,48,4,48]{5,3,1,0,2,4:T(8,128)(2,1)} %bitcast.26), kind=kLoop, calls=%fused_computation.18 | loop fusion | bytes 2359296 | tf_op jit(solution)/shard_map/slice | solution.py:263
  57.5 2.8 %copy.27 = bf16[1,8,4,48,4,48]{3,2,5,4,1,0:T(4,128)(2,1)S(1)} copy(bf16[1,8,4,48,4,48]{5,3,1,0,2,4:T(8,128)(2,1)} %get-tuple-element.12) | data formatting | bytes 1179648 | tf_op jit(solution)/shard_map/slice | solution.py:263
  60.3 0.9 squeeze.6
  61.1 2.6 %copy.28 = bf16[1,8,4,48,4,48]{5,4,3,2,1,0:T(4,128)(2,1)S(1)} copy(bf16[1,8,4,48,4,48]{5,3,1,0,2,4:T(8,128)(2,1)} %get-tuple-element.11) | data formatting | bytes 1179648 | tf_op jit(solution)/shard_map/slice | solution.py:263
  63.8 1.6 %squeeze.7 = bf16[8,192,192]{2,1,0:T(8,128)(2,1)} reshape(bf16[1,8,4,48,4,48]{5,4,3,2,1,0:T(4,128)(2,1)S(1)} %copy.28) | data formatting | bytes 1179648 | tf_op jit(solution)/shard_map/squeeze | solution.py:263
  65.4 1.5 %convolution_convert_fusion = bf16[8,192,192]{2,1,0:T(8,128)(2,1)S(1)} fusion(bf16[8,192,192]{1,2,0:T(8,128)(2,1)S(1)} %squeeze.6, bf16[8,192,192]{2,1,0:T(8,128)(2,1)} %squeeze.7), kind=kOutput, calls=%fused_computation | convolution fusion | flops 113541120 | bytes 1769472 | tf_op jit(solution)/shard_map/ckj,cki->cji/dot_general | solution.py:262
  66.9 0.4 copy.29
  67.3 0.0 copy-start
  67.4 0.3 copy.30
  67.7 0.7 reshape.94.out
  68.4 0.1 copy.31.out_gain
  68.5 0.1 copy.32.out_bias
  68.7 19.7 %finish.1 = bf16[2304,128]{1,0:T(8,128)(2,1)S(1)} custom-call(bf16[16,16,1152]{2,1,0:T(8,128)(2,1)S(1)} %reshape.94.out, bf16[2304,128]{1,0:T(8,128)(2,1)S(1)} %bitcast.21, f32[1,128]{1,0:T(1,128)S(1)} %bitcast.23, f32[1,128]{1,0:T(1,128)S(1)} %bitcast.25, f32[128,1]{1,0:T(8,128)S(1)} %copy.31.out_gain, f32[128,1]{1,0:T(8,128)S(1)} %copy.32.out_bias, ...), custom_call_target="tpu_custom_call" | custom-call | tf_op jit(solution)/shard_map/finish/pallas_call | solution.py:325
  88.4 0.8 copy.36
  (15 shorter events, 0.1 us)
Async XLA Ops:
  3.0 0.7 copy-start.2
  3.7 0.7 copy-start.4
  67.3 1.1 %copy-start.6 = (f32[128]{0:T(128)S(1)}, f32[128]{0:T(128)}, u32[]{:S(2)}) copy-start(f32[128]{0:T(128)} %param.20) | copy-start | bytes 1540
  67.3 1.2 %copy-start.7 = (f32[128]{0:T(128)S(1)}, f32[128]{0:T(128)}, u32[]{:S(2)}) copy-start(f32[128]{0:T(128)} %param.21) | copy-start | bytes 1540
  67.3 1.3 %copy-start = (bf16[128,128]{1,0:T(8,128)(2,1)S(1)}, bf16[128,128]{1,0:T(8,128)(2,1)}, u32[]{:S(2)}) copy-start(bf16[128,128]{1,0:T(8,128)(2,1)} %proj.1) | copy-start | bytes 98308
  67.4 1.3 %copy-start.1 = (bf16[128,128]{1,0:T(8,128)(2,1)S(1)}, bf16[128,128]{1,0:T(8,128)(2,1)}, u32[]{:S(2)}) copy-start(bf16[128,128]{1,0:T(8,128)(2,1)} %gate_w.1) | copy-start | bytes 98308
  67.4 1.3 %copy-start.3 = (f32[128]{0:T(128)S(1)}, f32[128]{0:T(128)}, u32[]{:S(2)}) copy-start(f32[128]{0:T(128)} %param.14) | copy-start | bytes 1540
  67.4 1.3 %copy-start.5 = (f32[128]{0:T(128)S(1)}, f32[128]{0:T(128)}, u32[]{:S(2)}) copy-start(f32[128]{0:T(128)} %param.15) | copy-start | bytes 1540

commit v2 on v0

--- a/solution.py
+++ b/solution.py
@@ -1,6 +1,10 @@
+import functools
+
 import jax
 import jax.numpy as jnp
 from jax import lax
+from jax.experimental import pallas as pl
+from jax.experimental.pallas import tpu as pltpu
 from jax.sharding import PartitionSpec as P
 
 EPS = 1e-05
@@ -29,7 +33,7 @@
     return (base_flat.astype(jnp.float32) + gate * update).astype(jnp.bfloat16)
 
 
-def shards(
+def shards_general(
     pair,
     chain_len,
     norm_gain,
@@ -87,6 +91,367 @@
     return relaid
 
 
+MESH = pl.DeviceIdType.MESH
+
+
+def place(rows, chans, subs):
+    row, chan, sub = lax.axis_index("row"), lax.axis_index("chan"), lax.axis_index("sub")
+    return (row * chans + chan) * subs + sub
+
+
+def coords(member, chans, subs):
+    return {
+        "row": member // (chans * subs),
+        "chan": (member // subs) % chans,
+        "sub": member % subs,
+    }
+
+
+def greet(me, count, chans, subs):
+    barrier = pltpu.get_barrier_semaphore()
+    for step in range(1, count):
+        peer = lax.rem(me + step, count)
+        pl.semaphore_signal(
+            barrier, inc=1, device_id=coords(peer, chans, subs), device_id_type=MESH
+        )
+    pl.semaphore_wait(barrier, count - 1)
+
+
+def norm_rows(values, gain, bias):
+    mean = jnp.mean(values, axis=1, keepdims=True)
+    centred = values - mean
+    spread = jnp.mean(centred * centred, axis=1, keepdims=True)
+    return centred * lax.rsqrt(spread + EPS) * gain + bias
+
+
+def residues_held(positions, chain_len, slot):
+    held = jnp.zeros(positions.shape, jnp.float32)
+    for chain in range(chain_len.shape[0]):
+        first = chain * slot
+        inside = (positions >= first) & (positions < first + chain_len[chain])
+        held = jnp.where(inside, 1.0, held)
+    return held
+
+
+def update_kernel(
+    dims,
+    chain_len,
+    pair,
+    params,
+    weights,
+    result,
+    out,
+    sides,
+    moved,
+    w_t,
+    picks,
+    spread,
+    tri_rows,
+    tri_out,
+    tri_got,
+    gates,
+    side_sems,
+    pair_sems,
+    tri_sems,
+    own_sems,
+):
+    rows, chans, subs = dims
+    blocks = chans * subs
+    count = rows * blocks
+    me = place(rows, chans, subs)
+    my_row = me // blocks
+    my_block = lax.rem(me, blocks)
+    greet(me, count, chans, subs)
+    width, height, depth = pair.shape
+    share = width // rows
+    slot = rows * height // chain_len.shape[0]
+    steps, lanes = out.shape[1], out.shape[3]
+    columns = lanes // height
+    hidden = weights.shape[2]
+    per = hidden // count
+    total = rows * height
+    sends = []
+
+    def remote(source, target, sems, device):
+        copy = pltpu.make_async_remote_copy(
+            src_ref=source,
+            dst_ref=target,
+            send_sem=sems[0],
+            recv_sem=sems[1],
+            device_id=device,
+            device_id_type=MESH,
+        )
+        copy.start()
+        sends.append(copy)
+        return copy
+
+    pair_waits = []
+    my_span = pl.ds(pl.multiple_of(my_row * height, height), height)
+
+    def send_pair(part):
+        size = share // 2
+        for step in range(1, rows):
+            target = lax.rem(my_row + step, rows)
+            pair_waits.append(
+                remote(
+                    pair.at[pl.ds(target * share + part * size, size)],
+                    moved.at[pl.ds(part * size, size), my_span],
+                    (pair_sems.at[0, part, step], pair_sems.at[1, part, step]),
+                    {"row": target},
+                )
+            )
+
+    own_pair = pltpu.make_async_copy(
+        pair.at[pl.ds(my_row * share, share)], moved.at[:, my_span], own_sems.at[0]
+    )
+    own_pair.start()
+    send_pair(0)
+    for index in range(4):
+        w_t[pl.ds(index * hidden, hidden)] = (
+            weights[index].astype(jnp.float32).T.astype(jnp.bfloat16)
+        )
+    gain, bias = params[0:1], params[1:2]
+    out_gain, out_bias = params[2:3], params[3:4]
+    lane = lax.broadcasted_iota(jnp.int32, (1, lanes), 1)
+    column = jnp.zeros((1, lanes), jnp.int32)
+    for edge in range(1, columns):
+        column = column + (lane >= edge * height).astype(jnp.int32)
+    row_held = residues_held(lane - column * height + my_row * height, chain_len, slot)
+
+    def side_body(index, carry):
+        block = pair[pl.ds(index * columns, columns)]
+        flat = block.astype(jnp.float32).reshape(lanes, depth)
+        normed = norm_rows(flat, gain, bias).astype(jnp.bfloat16)
+        projected = lax.dot_general(
+            w_t[...], normed, (((1,), (1,)), ((), ())), preferred_element_type=jnp.float32
+        )
+        held = residues_held(column + (my_block * width + index * columns), chain_len, slot)
+        valid = held * row_held
+        left = valid * jax.nn.sigmoid(projected[hidden : 2 * hidden]) * projected[:hidden]
+        right = (
+            valid * jax.nn.sigmoid(projected[3 * hidden :]) * projected[2 * hidden : 3 * hidden]
+        )
+        both = jnp.concatenate(
+            [left.reshape(count, per, lanes), right.reshape(count, per, lanes)], axis=1
+        )
+        out[:, index] = both.astype(jnp.bfloat16)
+        return carry
+
+    side_waits = []
+    my_lanes = pl.ds(pl.multiple_of(my_row * lanes, 128), lanes)
+    size = steps // 2
+    for piece in range(2):
+        lax.fori_loop(piece * size, (piece + 1) * size, side_body, 0)
+        span = pl.ds(piece * size, size)
+        for step in range(1, count):
+            peer = lax.rem(me + step, count)
+            side_waits.append(
+                remote(
+                    out.at[peer, span],
+                    sides.at[my_block, span, :, my_lanes],
+                    (side_sems.at[0, piece, step], side_sems.at[1, piece, step]),
+                    coords(peer, chans, subs),
+                )
+            )
+    own_side = pltpu.make_async_copy(
+        out.at[me], sides.at[my_block, :, :, my_lanes], own_sems.at[1]
+    )
+    own_side.start()
+    send_pair(1)
+
+    packed = lax.broadcasted_iota(jnp.int32, (lanes, 2 * 128), 0)
+    place_of = lax.broadcasted_iota(jnp.int32, (lanes, 2 * 128), 1)
+
+    def pick_body(index, carry):
+        at, row = index // rows, index % rows
+        low = row * height
+        hit = (packed - place_of == at * height - low) & (place_of >= low)
+        hit = hit & (place_of < low + height)
+        spot = pl.ds(pl.multiple_of(row * lanes, 128), lanes)
+        picks[at, spot] = jnp.where(hit, 1.0, 0.0).astype(jnp.bfloat16)
+        return carry
+
+    lax.fori_loop(0, columns * rows, pick_body, 0)
+    for copy in side_waits:
+        copy.wait_recv()
+    own_side.wait()
+
+    found = blocks * steps * 2 * per
+
+    def spread_body(index, carry):
+        held = jnp.dot(
+            sides[...].reshape(found, rows * lanes), picks[index], preferred_element_type=jnp.float32
+        )
+        spot = pl.ds(pl.multiple_of(index * found, 8), found)
+        spread[0, spot] = held[:, :128]
+        spread[1, spot] = held[:, 128:]
+        return carry
+
+    lax.fori_loop(0, columns, spread_body, 0)
+    depth_k = blocks * width
+
+    for channel in range(per):
+        def side(first):
+            spot = pl.ds(first, depth_k, stride=2 * per)
+            return jnp.concatenate([spread[0, spot, :], spread[1, spot, :]], axis=1).astype(
+                jnp.bfloat16
+            )
+
+        tri = lax.dot_general(
+            side(per + channel),
+            side(channel),
+            (((0,), (0,)), ((), ())),
+            preferred_element_type=jnp.float32,
+        )
+        spot = pl.ds(channel, total, stride=per)
+        tri_rows[0, spot, :] = tri[:total, :128]
+        tri_rows[1, spot, :] = tri[:total, 128:]
+
+    narrow = lax.broadcasted_iota(jnp.int32, (per, 128), 1) < 64
+    tri_waits = []
+    own_tri = []
+    for unit in range(share // 4):
+
+        def pack_body(index, carry):
+            halves = []
+            for half in range(2):
+                first = index * share + half * (share // 2) + 2 * unit
+                one = pl.ds(pl.multiple_of(first * per, per), per)
+                two = pl.ds(pl.multiple_of((first + 1) * per, per), per)
+                rest = jnp.where(narrow, tri_rows[1, one], pltpu.roll(tri_rows[1, two], 64, 1))
+                halves.append(jnp.concatenate([tri_rows[0, one], tri_rows[0, two], rest], axis=1))
+            tri_out[index, unit] = jnp.concatenate(halves, axis=0).astype(jnp.bfloat16)
+            return carry
+
+        lax.fori_loop(0, count, pack_body, 0)
+        arriving = []
+        for step in range(1, count):
+            peer = lax.rem(me + step, count)
+            arriving.append(
+                remote(
+                    tri_out.at[lax.rem(peer, blocks) * rows + peer // blocks, unit],
+                    tri_got.at[me, unit],
+                    (tri_sems.at[0, unit, step], tri_sems.at[1, unit, step]),
+                    coords(peer, chans, subs),
+                )
+            )
+        tri_waits.append(arriving)
+        own = pltpu.make_async_copy(
+            tri_out.at[my_block * rows + my_row, unit], tri_got.at[me, unit], own_sems.at[2 + unit]
+        )
+        own.start()
+        own_tri.append(own)
+
+    for copy in pair_waits:
+        copy.wait_recv()
+    own_pair.wait()
+
+    def base_of(half, unit):
+        first = half * (share // 2) + 2 * unit
+        return jnp.concatenate(
+            [
+                moved[first, :128],
+                moved[first + 1, :128],
+                moved[first, 128:],
+                moved[first + 1, 128:],
+            ],
+            axis=0,
+        ).astype(jnp.float32)
+
+    for unit in range(share // 4):
+        for half in range(2):
+            normed = norm_rows(base_of(half, unit), gain, bias).astype(jnp.bfloat16)
+            gates[unit, half] = jax.nn.sigmoid(
+                jnp.dot(normed, weights[5], preferred_element_type=jnp.float32)
+            )
+    for unit in range(share // 4):
+        for copy in tri_waits[unit]:
+            copy.wait_recv()
+        own_tri[unit].wait()
+        tri = tri_got[:, unit].astype(jnp.float32)
+        for half in range(2):
+            piece = tri[:, half * per : (half + 1) * per].reshape(hidden, 2 * total)
+            mean = jnp.mean(piece, axis=0, keepdims=True)
+            centred = piece - mean
+            square = jnp.mean(centred * centred, axis=0, keepdims=True)
+            scaled = (centred * lax.rsqrt(square + EPS)).T
+            tri_normed = (scaled * out_gain + out_bias).astype(jnp.bfloat16)
+            update = jnp.dot(tri_normed, weights[4], preferred_element_type=jnp.float32)
+            done = (base_of(half, unit) + gates[unit, half] * update).astype(jnp.bfloat16)
+            first = half * (share // 2) + 2 * unit
+            result[first, :128] = done[:128]
+            result[first + 1, :128] = done[128:256]
+            result[first, 128:] = done[256 : 128 + total]
+            result[first + 1, 128:] = done[128 + total :]
+    for copy in sends:
+        copy.wait_send()
+
+
+def shards_direct(pair, chain_len, *params):
+    height, width, depth = pair.shape
+    norm_gain, norm_bias, left_proj, left_gate, right_proj, right_gate = params[:6]
+    out_norm_gain, out_norm_bias, out_proj, out_gate = params[6:]
+    hidden = left_proj.shape[1]
+    dims = (lax.axis_size("row"), lax.axis_size("chan"), lax.axis_size("sub"))
+    blocks = dims[1] * dims[2]
+    count = dims[0] * blocks
+    per = hidden // count
+    total = height * dims[0]
+    share = width // dims[0]
+    columns = 8
+    lanes = columns * height
+    steps = width // columns
+    units = share // 4
+    vectors = jnp.stack([norm_gain, norm_bias, out_norm_gain, out_norm_bias])
+    weights = jnp.stack([left_proj, left_gate, right_proj, right_gate, out_proj, out_gate])
+    whole = pl.BlockSpec(memory_space=pltpu.VMEM)
+    result = pl.pallas_call(
+        functools.partial(update_kernel, dims),
+        out_shape=jax.ShapeDtypeStruct((share, total, depth), jnp.bfloat16),
+        in_specs=[pl.BlockSpec(memory_space=pltpu.SMEM)] + [whole] * 3,
+        out_specs=whole,
+        scratch_shapes=[
+            pltpu.VMEM((count, steps, 2 * per, lanes), jnp.bfloat16),
+            pltpu.VMEM((blocks, steps, 2 * per, dims[0] * lanes), jnp.bfloat16),
+            pltpu.VMEM((share, total, depth), jnp.bfloat16),
+            pltpu.VMEM((4 * hidden, depth), jnp.bfloat16),
+            pltpu.VMEM((columns, dims[0] * lanes, 256), jnp.bfloat16),
+            pltpu.VMEM((2, blocks * width * 2 * per, 128), jnp.float32),
+            pltpu.VMEM((2, total * per, 128), jnp.float32),
+            pltpu.VMEM((count, units, 2 * per, 2 * total), jnp.bfloat16),
+            pltpu.VMEM((count, units, 2 * per, 2 * total), jnp.bfloat16),
+            pltpu.VMEM((units, 2, 2 * total, depth), jnp.float32),
+            pltpu.SemaphoreType.DMA((2, 2, count)),
+            pltpu.SemaphoreType.DMA((2, 2, dims[0])),
+            pltpu.SemaphoreType.DMA((2, units, count)),
+            pltpu.SemaphoreType.DMA((2 + units,)),
+        ],
+        compiler_params=pltpu.CompilerParams(
+            collective_id=0, has_side_effects=True, vmem_limit_bytes=48 << 20
+        ),
+        name="update",
+    )(chain_len, pair.transpose(1, 0, 2), vectors, weights)
+    return result.transpose(1, 0, 2)
+
+
+def shards(pair, chain_len, *params):
+    height, width, _ = pair.shape
+    hidden = params[2].shape[1]
+    rows = lax.axis_size("row")
+    count = rows * lax.axis_size("chan") * lax.axis_size("sub")
+    fits = (
+        count * 8 == hidden
+        and height % 16 == 0
+        and (8 * height) % 128 == 0
+        and width % 16 == 0
+        and width % (4 * rows) == 0
+        and height * rows == 192
+        and width * count == 192 * rows
+    )
+    body = shards_direct if fits else shards_general
+    return body(pair, chain_len, *params)
+
+
 def solution(mesh):
     return jax.shard_map(
         shards,

time: 159 us -> 70.4 us (0.44)
  Pallas kernels: 0 us -> 62.7 us
  waiting for transfers between devices: 52.4 us -> 0 us
  blocking collectives: 43.9 us -> 0 us
  local copies, waits for them, and re-layouts: 30.4 us -> 7.19 us
  between operations: 13.7 us -> 0.04 us
  matrix products: 7.49 us -> 0 us
  other arithmetic: 7 us -> 0.01 us
  starting transfers between devices: 3.51 us -> 0 us
    pallas_call x0 -> x1, Pallas kernels: none -> 62.7 us  [shards_direct(): pl.pallas_call(functools.partial(update_kernel, dims), out_shape=jax.Shap...]
    all_gather x1 -> x0, waiting for transfers between devices: 44.4 us -> none  [shards(): lax.all_gather(right_c, 'row', axis=1, tiled=True)]
    all_to_all x3 -> x0, blocking collectives: 43.9 us -> none  [the longest x1 18.4 us: shards(): lax.all_to_all(result.reshape(rows, width, chans), 'row', split_axis=1, c...]
    all_to_all x1 -> x0, waiting for transfers between devices: 8.01 us -> none  [shards(): lax.all_to_all(tri, ('chan', 'sub'), split_axis=2, concat_axis=0, tiled=T...]
    unnamed x36 -> x27, local copies, waits for them, and re-layouts: 15.1 us -> 7.18 us
    dot_general x4 -> x0, matrix products: 7.49 us -> none  [the longest x1 2.99 us: shards(): jnp.einsum('cik,cjk->cij', left_c, lax.all_gather(right_c, 'row', axis=1,...]
    convert_element_type x5 -> x0, local copies, waits for them, and re-layouts: 7.08 us -> none  [the longest x2 5.03 us: finish(): tri_flat.astype(jnp.float32)]
    all_to_all x5 -> x0, local copies, waits for them, and re-layouts: 5.75 us -> none  [the longest x2 2.8 us: shards(): lax.all_to_all(right_t, ('chan', 'sub'), split_axis=0, concat_axis=2, til...]
  transfers between devices with their start and end apart: 2 -> 0, of which waited for: 2 -> 0; matrix products, arithmetic and copies ran while one was open for 5% -> 0% of each run, Pallas kernels for 0% -> 0%
where the time goes in v2:
time: 70.4 us; the launch traced here: 69.9 us
  Pallas kernels  62.7 us (89%)
  local copies, waits for them, and re-layouts  7.19 us (10%)
    pallas_call x1, Pallas kernels, shards_direct(): pl.pallas_call(functools.partial(update_kernel, dims), out_shape=jax.Shap...  62.7 us
    unnamed x27, local copies, waits for them, and re-layouts  7.18 us

profile of v2, /device:TPU:0, one launch (start us, length us, event | category | flops | bytes accessed | tf_op | source)
XLA Modules:
  0.0 69.9 jit_solution(7277498678072176928)
XLA Ops:
  0.0 0.0 copy-start.9
  0.0 0.0 copy-start.6
  0.0 0.0 copy-start.7
  0.0 0.0 copy-start.8
  0.0 0.6 copy-done.9
  0.7 0.0 copy-done.6
  0.7 0.0 copy-done.7
  0.7 0.0 copy-done.8
  0.7 0.0 copy-start.1
  0.7 0.8 %bitcast_dynamic-update-slice_fusion.5 = bf16[6,128,128]{2,1,0:T(8,128)(2,1)S(1)} fusion(bf16[128,128]{1,0:T(8,128)(2,1)} %param.16), kind=kLoop, calls=%fused_computation.6 | loop fusion | bytes 65536
  1.5 0.0 copy-done.1
  1.5 0.0 copy-start.2
  1.5 0.7 %copy-done.2 = bf16[128,128]{1,0:T(8,128)(2,1)S(1)} copy-done((bf16[128,128]{1,0:T(8,128)(2,1)S(1)}, bf16[128,128]{1,0:T(8,128)(2,1)}, u32[]{:S(2)}) %copy-start.2) | copy-done | bytes 32792
  2.3 0.0 copy-start.3
  2.3 0.7 %copy-done.3 = bf16[128,128]{1,0:T(8,128)(2,1)S(1)} copy-done((bf16[128,128]{1,0:T(8,128)(2,1)S(1)}, bf16[128,128]{1,0:T(8,128)(2,1)}, u32[]{:S(2)}) %copy-start.3) | copy-done | bytes 32792
  3.0 0.0 copy-start.4
  3.0 0.7 %copy-done.4 = bf16[128,128]{1,0:T(8,128)(2,1)S(1)} copy-done((bf16[128,128]{1,0:T(8,128)(2,1)S(1)}, bf16[128,128]{1,0:T(8,128)(2,1)}, u32[]{:S(2)}) %copy-start.4) | copy-done | bytes 32792
  3.8 0.0 copy-start.5
  3.8 0.7 %copy-done.5 = bf16[128,128]{1,0:T(8,128)(2,1)S(1)} copy-done((bf16[128,128]{1,0:T(8,128)(2,1)S(1)}, bf16[128,128]{1,0:T(8,128)(2,1)}, u32[]{:S(2)}) %copy-start.5) | copy-done | bytes 32792
  4.5 1.2 %copy.15 = bf16[48,48,128]{2,0,1:T(8,128)(2,1)S(1)} copy(bf16[48,48,128]{2,1,0:T(8,128)(2,1)} %param.12) | data formatting | bytes 1179648 | tf_op args[0]
  5.8 0.0 copy-start
  5.8 0.6 copy-done
  6.4 62.7 %update.1 = bf16[12,192,128]{2,1,0:T(8,128)(2,1)S(1)} custom-call(s32[4]{0:T(128)S(1)} %copy-done, bf16[48,48,128]{2,1,0:T(8,128)(2,1)S(1)} %bitcast.21, f32[4,128]{1,0:T(4,128)S(1)} %pad_maximum_fusion.params, bf16[6,128,128]{2,1,0:T(8,128)(2,1)S(1)} %bitcast_dynamic-update-slice_fusion.weights), custom_call_target="tpu_custom_call" | custom-call | tf_op jit(solution)/shard_map/update/pallas_call | solution.py:408
  69.1 0.8 %copy.22 = bf16[192,12,128]{2,0,1:T(8,128)(2,1)} copy(bf16[192,12,128]{2,0,1:T(8,128)(2,1)S(1)} %bitcast.20) | data formatting | bytes 1179648
  (6 shorter events, 0.1 us)
Async XLA Ops:
  0.0 0.7 copy-start.9
  0.0 0.7 copy-start.6
  0.0 0.7 copy-start.7
  0.0 0.7 copy-start.8
  0.7 0.8 %copy-start.1 = (bf16[128,128]{1,0:T(8,128)(2,1)S(1)}, bf16[128,128]{1,0:T(8,128)(2,1)}, u32[]{:S(2)}) copy-start(bf16[128,128]{1,0:T(8,128)(2,1)} %param.17) | copy-start | bytes 98308
  1.5 0.8 %copy-start.2 = (bf16[128,128]{1,0:T(8,128)(2,1)S(1)}, bf16[128,128]{1,0:T(8,128)(2,1)}, u32[]{:S(2)}) copy-start(bf16[128,128]{1,0:T(8,128)(2,1)} %param.18) | copy-start | bytes 98308
  2.3 0.8 %copy-start.3 = (bf16[128,128]{1,0:T(8,128)(2,1)S(1)}, bf16[128,128]{1,0:T(8,128)(2,1)}, u32[]{:S(2)}) copy-start(bf16[128,128]{1,0:T(8,128)(2,1)} %param.19) | copy-start | bytes 98308
  3.0 0.8 %copy-start.4 = (bf16[128,128]{1,0:T(8,128)(2,1)S(1)}, bf16[128,128]{1,0:T(8,128)(2,1)}, u32[]{:S(2)}) copy-start(bf16[128,128]{1,0:T(8,128)(2,1)} %param.22) | copy-start | bytes 98308
  3.8 0.8 %copy-start.5 = (bf16[128,128]{1,0:T(8,128)(2,1)S(1)}, bf16[128,128]{1,0:T(8,128)(2,1)}, u32[]{:S(2)}) copy-start(bf16[128,128]{1,0:T(8,128)(2,1)} %param.23) | copy-start | bytes 98308
  5.8 0.7 copy-start

commit v3 on v2

--- a/solution.py
+++ b/solution.py
@@ -137,9 +137,20 @@
     dims,
     chain_len,
     pair,
+    *refs,
+):
+    held_far, refs = refs[:10], refs[10:]
+    update_body(dims, chain_len, pair, held_far, *refs)
+
+
+def update_body(
+    dims,
+    chain_len,
+    pair,
+    held_far,
+    result,
     params,
     weights,
-    result,
     out,
     sides,
     moved,
@@ -154,11 +165,18 @@
     pair_sems,
     tri_sems,
     own_sems,
+    own_sides,
+    load_sems,
 ):
     rows, chans, subs = dims
     blocks = chans * subs
     count = rows * blocks
     me = place(rows, chans, subs)
+    loads = []
+    for index, source in enumerate(held_far):
+        target = params.at[index] if index < 4 else weights.at[index - 4]
+        loads.append(pltpu.make_async_copy(source, target, load_sems.at[index]))
+        loads[-1].start()
     my_row = me // blocks
     my_block = lax.rem(me, blocks)
     greet(me, count, chans, subs)
@@ -171,6 +189,13 @@
     per = hidden // count
     total = rows * height
     sends = []
+    offsets = [rows // 2] + [step for step in range(rows - 1, 0, -1) if step != rows // 2] + [0]
+    peers = []
+    for row_step in offsets:
+        for block_step in range(blocks):
+            if row_step or block_step:
+                row = lax.rem(my_row + row_step, rows)
+                peers.append((row, lax.rem(my_block + block_step, blocks)))
 
     def remote(source, target, sems, device):
         copy = pltpu.make_async_remote_copy(
@@ -190,7 +215,7 @@
 
     def send_pair(part):
         size = share // 2
-        for step in range(1, rows):
+        for step in offsets[:-1]:
             target = lax.rem(my_row + step, rows)
             pair_waits.append(
                 remote(
@@ -206,12 +231,13 @@
     )
     own_pair.start()
     send_pair(0)
+    for load in loads:
+        load.wait()
     for index in range(4):
         w_t[pl.ds(index * hidden, hidden)] = (
             weights[index].astype(jnp.float32).T.astype(jnp.bfloat16)
         )
-    gain, bias = params[0:1], params[1:2]
-    out_gain, out_bias = params[2:3], params[3:4]
+    gain, bias, out_gain, out_bias = (params[index] for index in range(4))
     lane = lax.broadcasted_iota(jnp.int32, (1, lanes), 1)
     column = jnp.zeros((1, lanes), jnp.int32)
     for edge in range(1, columns):
@@ -237,26 +263,28 @@
         out[:, index] = both.astype(jnp.bfloat16)
         return carry
 
-    side_waits = []
+    side_waits, own_side = [], []
     my_lanes = pl.ds(pl.multiple_of(my_row * lanes, 128), lanes)
     size = steps // 2
     for piece in range(2):
         lax.fori_loop(piece * size, (piece + 1) * size, side_body, 0)
         span = pl.ds(piece * size, size)
-        for step in range(1, count):
-            peer = lax.rem(me + step, count)
-            side_waits.append(
+        arriving = []
+        for step, (row, block) in enumerate(peers):
+            arriving.append(
                 remote(
-                    out.at[peer, span],
-                    sides.at[my_block, span, :, my_lanes],
+                    out.at[row * blocks + block, span],
+                    sides.at[piece, my_block, :, :, my_lanes],
                     (side_sems.at[0, piece, step], side_sems.at[1, piece, step]),
-                    coords(peer, chans, subs),
+                    coords(row * blocks + block, chans, subs),
                 )
             )
-    own_side = pltpu.make_async_copy(
-        out.at[me], sides.at[my_block, :, :, my_lanes], own_sems.at[1]
-    )
-    own_side.start()
+        side_waits.append(arriving)
+        own = pltpu.make_async_copy(
+            out.at[me, span], sides.at[piece, my_block, :, :, my_lanes], own_sides.at[piece]
+        )
+        own.start()
+        own_side.append(own)
     send_pair(1)
 
     packed = lax.broadcasted_iota(jnp.int32, (lanes, 2 * 128), 0)
@@ -272,22 +300,24 @@
         return carry
 
     lax.fori_loop(0, columns * rows, pick_body, 0)
-    for copy in side_waits:
-        copy.wait_recv()
-    own_side.wait()
-
-    found = blocks * steps * 2 * per
-
-    def spread_body(index, carry):
-        held = jnp.dot(
-            sides[...].reshape(found, rows * lanes), picks[index], preferred_element_type=jnp.float32
-        )
-        spot = pl.ds(pl.multiple_of(index * found, 8), found)
-        spread[0, spot] = held[:, :128]
-        spread[1, spot] = held[:, 128:]
-        return carry
-
-    lax.fori_loop(0, columns, spread_body, 0)
+    found = blocks * size * 2 * per
+    for piece in range(2):
+        for copy in side_waits[piece]:
+            copy.wait_recv()
+        own_side[piece].wait()
+
+        def spread_body(index, carry):
+            held = jnp.dot(
+                sides[piece].reshape(found, rows * lanes),
+                picks[index],
+                preferred_element_type=jnp.float32,
+            )
+            spot = pl.ds(pl.multiple_of((piece * columns + index) * found, 8), found)
+            spread[0, spot] = held[:, :128]
+            spread[1, spot] = held[:, 128:]
+            return carry
+
+        lax.fori_loop(0, columns, spread_body, 0)
     depth_k = blocks * width
 
     for channel in range(per):
@@ -325,14 +355,13 @@
 
         lax.fori_loop(0, count, pack_body, 0)
         arriving = []
-        for step in range(1, count):
-            peer = lax.rem(me + step, count)
+        for step, (row, block) in enumerate(peers):
             arriving.append(
                 remote(
-                    tri_out.at[lax.rem(peer, blocks) * rows + peer // blocks, unit],
+                    tri_out.at[block * rows + row, unit],
                     tri_got.at[me, unit],
                     (tri_sems.at[0, unit, step], tri_sems.at[1, unit, step]),
-                    coords(peer, chans, subs),
+                    coords(row * blocks + block, chans, subs),
                 )
             )
         tri_waits.append(arriving)
@@ -389,9 +418,7 @@
 
 def shards_direct(pair, chain_len, *params):
     height, width, depth = pair.shape
-    norm_gain, norm_bias, left_proj, left_gate, right_proj, right_gate = params[:6]
-    out_norm_gain, out_norm_bias, out_proj, out_gate = params[6:]
-    hidden = left_proj.shape[1]
+    hidden = params[2].shape[1]
     dims = (lax.axis_size("row"), lax.axis_size("chan"), lax.axis_size("sub"))
     blocks = dims[1] * dims[2]
     count = dims[0] * blocks
@@ -402,17 +429,20 @@
     lanes = columns * height
     steps = width // columns
     units = share // 4
-    vectors = jnp.stack([norm_gain, norm_bias, out_norm_gain, out_norm_bias])
-    weights = jnp.stack([left_proj, left_gate, right_proj, right_gate, out_proj, out_gate])
+    vectors = [vector[None, :] for vector in params[:2] + params[6:8]]
+    weights = params[2:6] + params[8:]
+    far = pl.BlockSpec(memory_space=pl.ANY)
     whole = pl.BlockSpec(memory_space=pltpu.VMEM)
     result = pl.pallas_call(
         functools.partial(update_kernel, dims),
         out_shape=jax.ShapeDtypeStruct((share, total, depth), jnp.bfloat16),
-        in_specs=[pl.BlockSpec(memory_space=pltpu.SMEM)] + [whole] * 3,
+        in_specs=[pl.BlockSpec(memory_space=pltpu.SMEM)] + [whole] + [far] * 10,
         out_specs=whole,
         scratch_shapes=[
+            pltpu.VMEM((4, 1, depth), jnp.float32),
+            pltpu.VMEM((6, depth, hidden), jnp.bfloat16),
             pltpu.VMEM((count, steps, 2 * per, lanes), jnp.bfloat16),
-            pltpu.VMEM((blocks, steps, 2 * per, dims[0] * lanes), jnp.bfloat16),
+            pltpu.VMEM((2, blocks, steps // 2, 2 * per, dims[0] * lanes), jnp.bfloat16),
             pltpu.VMEM((share, total, depth), jnp.bfloat16),
             pltpu.VMEM((4 * hidden, depth), jnp.bfloat16),
             pltpu.VMEM((columns, dims[0] * lanes, 256), jnp.bfloat16),
@@ -425,12 +455,14 @@
             pltpu.SemaphoreType.DMA((2, 2, dims[0])),
             pltpu.SemaphoreType.DMA((2, units, count)),
             pltpu.SemaphoreType.DMA((2 + units,)),
+            pltpu.SemaphoreType.DMA((2,)),
+            pltpu.SemaphoreType.DMA((10,)),
         ],
         compiler_params=pltpu.CompilerParams(
             collective_id=0, has_side_effects=True, vmem_limit_bytes=48 << 20
         ),
         name="update",
-    )(chain_len, pair.transpose(1, 0, 2), vectors, weights)
+    )(chain_len, pair.transpose(1, 0, 2), *vectors, *weights)
     return result.transpose(1, 0, 2)
 
 

time: 70.4 us -> 67.3 us (0.956)
  local copies, waits for them, and re-layouts: 7.19 us -> 2.73 us
  Pallas kernels: 62.7 us -> 64.3 us
    unnamed x27 -> x24, local copies, waits for them, and re-layouts: 7.18 us -> 2.73 us
    pallas_call x1, Pallas kernels: 62.7 us -> 64.3 us  [shards_direct(): pl.pallas_call(functools.partial(update_kernel, dims), out_shape=jax.Shap...]
where the time goes in v3:
time: 67.3 us; the launch traced here: 67.1 us
  Pallas kernels  64.3 us (96%)
  local copies, waits for them, and re-layouts  2.73 us (4%)
    pallas_call x1, Pallas kernels, shards_direct(): pl.pallas_call(functools.partial(update_kernel, dims), out_shape=jax.Shap...  64.3 us
    unnamed x24, local copies, waits for them, and re-layouts  2.73 us

profile of v3, /device:TPU:0, one launch (start us, length us, event | category | flops | bytes accessed | tf_op | source)
XLA Modules:
  0.0 67.1 jit_solution(4673244444620656129)
XLA Ops:
  0.0 0.0 copy-start
  0.0 0.0 copy-start.1
  0.0 0.0 copy-start.2
  0.0 0.0 copy-start.3
  0.0 0.0 copy-start.5
  0.0 0.0 copy-start.9
  0.0 0.0 copy-start.10
  0.0 1.3 %copy.15 = bf16[48,48,128]{2,0,1:T(8,128)(2,1)S(1)} copy(bf16[48,48,128]{2,1,0:T(8,128)(2,1)} %param.12) | data formatting | bytes 1179648 | tf_op args[0]
  1.3 0.0 copy-start.6
  1.4 0.0 copy-start.7
  1.4 0.0 copy-start.8
  1.4 0.0 copy-done
  1.4 0.0 copy-done.1
  1.4 0.0 copy-done.2
  1.4 0.0 copy-done.3
  1.4 0.0 copy-done.4
  1.4 0.0 copy-done.5
  1.4 0.0 copy-done.9
  1.5 0.0 copy-done.10
  1.5 0.5 copy-done.6
  2.0 0.0 copy-done.7
  2.0 0.0 copy-done.8
  2.0 64.3 %update.1 = bf16[12,192,128]{2,1,0:T(8,128)(2,1)S(1)} custom-call(s32[4]{0:T(128)S(1)} %copy-done.6, bf16[48,48,128]{2,1,0:T(8,128)(2,1)S(1)} %bitcast.9, f32[1,128]{1,0:T(1,128)S(1)} %bitcast.10, f32[1,128]{1,0:T(1,128)S(1)} %bitcast.11, f32[1,128]{1,0:T(1,128)S(1)} %bitcast.12, f32[1,128]{1,0:T(1,128)S(1)} %bitcast.13, bf16[128,128]{1,0:T(8,128)(2,1)S(1)} %copy-done, ...), custom_call_target="tpu_custom_call" | custom-call | tf_op jit(solution)/shard_map/update/pallas_call | solution.py:436
  66.3 0.8 %copy.17 = bf16[192,12,128]{2,0,1:T(8,128)(2,1)} copy(bf16[192,12,128]{2,0,1:T(8,128)(2,1)S(1)} %bitcast.8) | data formatting | bytes 1179648
  (1 shorter events, 0.0 us)
Async XLA Ops:
  0.0 1.4 %copy-start = (bf16[128,128]{1,0:T(8,128)(2,1)S(1)}, bf16[128,128]{1,0:T(8,128)(2,1)}, u32[]{:S(2)}) copy-start(bf16[128,128]{1,0:T(8,128)(2,1)} %refs_4_.1) | copy-start | bytes 98308
  0.0 1.4 %copy-start.1 = (bf16[128,128]{1,0:T(8,128)(2,1)S(1)}, bf16[128,128]{1,0:T(8,128)(2,1)}, u32[]{:S(2)}) copy-start(bf16[128,128]{1,0:T(8,128)(2,1)} %refs_5_.1) | copy-start | bytes 98308
  0.0 1.4 %copy-start.2 = (bf16[128,128]{1,0:T(8,128)(2,1)S(1)}, bf16[128,128]{1,0:T(8,128)(2,1)}, u32[]{:S(2)}) copy-start(bf16[128,128]{1,0:T(8,128)(2,1)} %refs_6_.1) | copy-start | bytes 98308
  0.0 1.4 %copy-start.3 = (bf16[128,128]{1,0:T(8,128)(2,1)S(1)}, bf16[128,128]{1,0:T(8,128)(2,1)}, u32[]{:S(2)}) copy-start(bf16[128,128]{1,0:T(8,128)(2,1)} %refs_7_.1) | copy-start | bytes 98308
  0.0 1.4 %copy-start.4 = (bf16[128,128]{1,0:T(8,128)(2,1)S(1)}, bf16[128,128]{1,0:T(8,128)(2,1)}, u32[]{:S(2)}) copy-start(bf16[128,128]{1,0:T(8,128)(2,1)} %refs_8_.1) | copy-start | bytes 98308
  0.0 1.4 %copy-start.5 = (bf16[128,128]{1,0:T(8,128)(2,1)S(1)}, bf16[128,128]{1,0:T(8,128)(2,1)}, u32[]{:S(2)}) copy-start(bf16[128,128]{1,0:T(8,128)(2,1)} %refs_9_.1) | copy-start | bytes 98308
  0.0 1.4 %copy-start.9 = (f32[128]{0:T(128)S(1)}, f32[128]{0:T(128)}, u32[]{:S(2)}) copy-start(f32[128]{0:T(128)} %param.20) | copy-start | bytes 1540
  0.0 1.4 %copy-start.10 = (f32[128]{0:T(128)S(1)}, f32[128]{0:T(128)}, u32[]{:S(2)}) copy-start(f32[128]{0:T(128)} %param.21) | copy-start | bytes 1540
  1.3 0.7 copy-start.6
  1.4 0.7 copy-start.7
  1.4 0.7 copy-start.8

commit v4 on v3

--- a/solution.py
+++ b/solution.py
@@ -114,7 +114,7 @@
         pl.semaphore_signal(
             barrier, inc=1, device_id=coords(peer, chans, subs), device_id_type=MESH
         )
-    pl.semaphore_wait(barrier, count - 1)
+    return barrier
 
 
 def norm_rows(values, gain, bias):
@@ -179,7 +179,7 @@
         loads[-1].start()
     my_row = me // blocks
     my_block = lax.rem(me, blocks)
-    greet(me, count, chans, subs)
+    barrier = greet(me, count, chans, subs)
     width, height, depth = pair.shape
     share = width // rows
     slot = rows * height // chain_len.shape[0]
@@ -230,7 +230,6 @@
         pair.at[pl.ds(my_row * share, share)], moved.at[:, my_span], own_sems.at[0]
     )
     own_pair.start()
-    send_pair(0)
     for load in loads:
         load.wait()
     for index in range(4):
@@ -265,9 +264,12 @@
 
     side_waits, own_side = [], []
     my_lanes = pl.ds(pl.multiple_of(my_row * lanes, 128), lanes)
-    size = steps // 2
-    for piece in range(2):
+    pieces = sides.shape[0]
+    size = steps // pieces
+    for piece in range(pieces):
         lax.fori_loop(piece * size, (piece + 1) * size, side_body, 0)
+        if piece == 0:
+            pl.semaphore_wait(barrier, count - 1)
         span = pl.ds(piece * size, size)
         arriving = []
         for step, (row, block) in enumerate(peers):
@@ -285,8 +287,8 @@
         )
         own.start()
         own_side.append(own)
-    send_pair(1)
-
+
+    send_pair(0)
     packed = lax.broadcasted_iota(jnp.int32, (lanes, 2 * 128), 0)
     place_of = lax.broadcasted_iota(jnp.int32, (lanes, 2 * 128), 1)
 
@@ -301,10 +303,12 @@
 
     lax.fori_loop(0, columns * rows, pick_body, 0)
     found = blocks * size * 2 * per
-    for piece in range(2):
+    for piece in range(pieces):
         for copy in side_waits[piece]:
             copy.wait_recv()
         own_side[piece].wait()
+        if piece == pieces - 1:
+            send_pair(1)
 
         def spread_body(index, carry):
             held = jnp.dot(
@@ -429,6 +433,7 @@
     lanes = columns * height
     steps = width // columns
     units = share // 4
+    pieces = 3
     vectors = [vector[None, :] for vector in params[:2] + params[6:8]]
     weights = params[2:6] + params[8:]
     far = pl.BlockSpec(memory_space=pl.ANY)
@@ -442,7 +447,7 @@
             pltpu.VMEM((4, 1, depth), jnp.float32),
             pltpu.VMEM((6, depth, hidden), jnp.bfloat16),
             pltpu.VMEM((count, steps, 2 * per, lanes), jnp.bfloat16),
-            pltpu.VMEM((2, blocks, steps // 2, 2 * per, dims[0] * lanes), jnp.bfloat16),
+            pltpu.VMEM((pieces, blocks, steps // pieces, 2 * per, dims[0] * lanes), jnp.bfloat16),
             pltpu.VMEM((share, total, depth), jnp.bfloat16),
             pltpu.VMEM((4 * hidden, depth), jnp.bfloat16),
             pltpu.VMEM((columns, dims[0] * lanes, 256), jnp.bfloat16),
@@ -451,11 +456,11 @@
             pltpu.VMEM((count, units, 2 * per, 2 * total), jnp.bfloat16),
             pltpu.VMEM((count, units, 2 * per, 2 * total), jnp.bfloat16),
             pltpu.VMEM((units, 2, 2 * total, depth), jnp.float32),
-            pltpu.SemaphoreType.DMA((2, 2, count)),
+            pltpu.SemaphoreType.DMA((2, pieces, count)),
             pltpu.SemaphoreType.DMA((2, 2, dims[0])),
             pltpu.SemaphoreType.DMA((2, units, count)),
             pltpu.SemaphoreType.DMA((2 + units,)),
-            pltpu.SemaphoreType.DMA((2,)),
+            pltpu.SemaphoreType.DMA((pieces,)),
             pltpu.SemaphoreType.DMA((10,)),
         ],
         compiler_params=pltpu.CompilerParams(
@@ -475,7 +480,7 @@
         count * 8 == hidden
         and height % 16 == 0
         and (8 * height) % 128 == 0
-        and width % 16 == 0
+        and width % 24 == 0
         and width % (4 * rows) == 0
         and height * rows == 192
         and width * count == 192 * rows

time: 67.3 us -> 63.8 us (0.948)
  Pallas kernels: 64.3 us -> 60.8 us
    pallas_call x1, Pallas kernels: 64.3 us -> 60.8 us  [shards_direct(): pl.pallas_call(functools.partial(update_kernel, dims), out_shape=jax.Shap...]
where the time goes in v4:
time: 63.8 us; the launch traced here: 63.6 us
  Pallas kernels  60.8 us (95%)
  local copies, waits for them, and re-layouts  2.73 us (4%)
    pallas_call x1, Pallas kernels, shards_direct(): pl.pallas_call(functools.partial(update_kernel, dims), out_shape=jax.Shap...  60.8 us
    unnamed x24, local copies, waits for them, and re-layouts  2.73 us

profile of v4, /device:TPU:0, one launch (start us, length us, event | category | flops | bytes accessed | tf_op | source)
XLA Modules:
  0.0 63.6 jit_solution(2543970061093022109)
XLA Ops:
  0.0 0.0 copy-start
  0.0 0.0 copy-start.1
  0.0 0.0 copy-start.2
  0.0 0.0 copy-start.3
  0.0 0.0 copy-start.5
  0.0 0.0 copy-start.9
  0.0 0.0 copy-start.10
  0.0 1.3 %copy.15 = bf16[48,48,128]{2,0,1:T(8,128)(2,1)S(1)} copy(bf16[48,48,128]{2,1,0:T(8,128)(2,1)} %param.12) | data formatting | bytes 1179648 | tf_op args[0]
  1.3 0.0 copy-start.6
  1.4 0.0 copy-start.7
  1.4 0.0 copy-start.8
  1.4 0.0 copy-done
  1.4 0.0 copy-done.1
  1.4 0.0 copy-done.2
  1.4 0.0 copy-done.3
  1.4 0.0 copy-done.4
  1.4 0.0 copy-done.5
  1.4 0.0 copy-done.9
  1.5 0.0 copy-done.10
  1.5 0.5 copy-done.6
  2.0 0.0 copy-done.7
  2.0 0.0 copy-done.8
  2.0 60.8 %update.1 = bf16[12,192,128]{2,1,0:T(8,128)(2,1)S(1)} custom-call(s32[4]{0:T(128)S(1)} %copy-done.6, bf16[48,48,128]{2,1,0:T(8,128)(2,1)S(1)} %bitcast.9, f32[1,128]{1,0:T(1,128)S(1)} %bitcast.10, f32[1,128]{1,0:T(1,128)S(1)} %bitcast.11, f32[1,128]{1,0:T(1,128)S(1)} %bitcast.12, f32[1,128]{1,0:T(1,128)S(1)} %bitcast.13, bf16[128,128]{1,0:T(8,128)(2,1)S(1)} %copy-done, ...), custom_call_target="tpu_custom_call" | custom-call | tf_op jit(solution)/shard_map/update/pallas_call | solution.py:441
  62.8 0.8 %copy.17 = bf16[192,12,128]{2,0,1:T(8,128)(2,1)} copy(bf16[192,12,128]{2,0,1:T(8,128)(2,1)S(1)} %bitcast.8) | data formatting | bytes 1179648
  (1 shorter events, 0.0 us)
Async XLA Ops:
  0.0 1.4 %copy-start = (bf16[128,128]{1,0:T(8,128)(2,1)S(1)}, bf16[128,128]{1,0:T(8,128)(2,1)}, u32[]{:S(2)}) copy-start(bf16[128,128]{1,0:T(8,128)(2,1)} %refs_4_.1) | copy-start | bytes 98308
  0.0 1.4 %copy-start.1 = (bf16[128,128]{1,0:T(8,128)(2,1)S(1)}, bf16[128,128]{1,0:T(8,128)(2,1)}, u32[]{:S(2)}) copy-start(bf16[128,128]{1,0:T(8,128)(2,1)} %refs_5_.1) | copy-start | bytes 98308
  0.0 1.4 %copy-start.2 = (bf16[128,128]{1,0:T(8,128)(2,1)S(1)}, bf16[128,128]{1,0:T(8,128)(2,1)}, u32[]{:S(2)}) copy-start(bf16[128,128]{1,0:T(8,128)(2,1)} %refs_6_.1) | copy-start | bytes 98308
  0.0 1.4 %copy-start.3 = (bf16[128,128]{1,0:T(8,128)(2,1)S(1)}, bf16[128,128]{1,0:T(8,128)(2,1)}, u32[]{:S(2)}) copy-start(bf16[128,128]{1,0:T(8,128)(2,1)} %refs_7_.1) | copy-start | bytes 98308
  0.0 1.4 %copy-start.4 = (bf16[128,128]{1,0:T(8,128)(2,1)S(1)}, bf16[128,128]{1,0:T(8,128)(2,1)}, u32[]{:S(2)}) copy-start(bf16[128,128]{1,0:T(8,128)(2,1)} %refs_8_.1) | copy-start | bytes 98308
  0.0 1.4 %copy-start.5 = (bf16[128,128]{1,0:T(8,128)(2,1)S(1)}, bf16[128,128]{1,0:T(8,128)(2,1)}, u32[]{:S(2)}) copy-start(bf16[128,128]{1,0:T(8,128)(2,1)} %refs_9_.1) | copy-start | bytes 98308
  0.0 1.4 %copy-start.9 = (f32[128]{0:T(128)S(1)}, f32[128]{0:T(128)}, u32[]{:S(2)}) copy-start(f32[128]{0:T(128)} %param.20) | copy-start | bytes 1540
  0.0 1.4 %copy-start.10 = (f32[128]{0:T(128)S(1)}, f32[128]{0:T(128)}, u32[]{:S(2)}) copy-start(f32[128]{0:T(128)} %param.21) | copy-start | bytes 1540
  1.3 0.7 %copy-start.6 = (s32[4]{0:T(128)S(1)}, s32[4]{0:T(128)}, u32[]{:S(2)}) copy-start(s32[4]{0:T(128)} %chain_len.1) | copy-start | bytes 52
  1.4 0.7 %copy-start.7 = (f32[128]{0:T(128)S(1)}, f32[128]{0:T(128)}, u32[]{:S(2)}) copy-start(f32[128]{0:T(128)} %param.14) | copy-start | bytes 1540
  1.4 0.7 %copy-start.8 = (f32[128]{0:T(128)S(1)}, f32[128]{0:T(128)}, u32[]{:S(2)}) copy-start(f32[128]{0:T(128)} %param.15) | copy-start | bytes 1540
